TPU v7x, 256 devices: a whole 4x4x8 slice. The times are simulated.
256 devices in a mesh: var: 32 (over z_lo, x, core), tp: 8 (over z_hi, y).
Axes of the slice: x: 4, y: 4, z: 8 (z_hi: 2, z_lo: 4; z = z_hi * 4 + z_lo), core: 2. Of those that a mesh axis runs over, the one named last changes fastest.
Arguments:
- parent_inputs: bfloat16 [4096, 256], P('var'), may hold values from -6 to 6
- gate_parent: bfloat16 [4096, 7168], P('var', 'tp'), may hold values from -0.09375 to 0.09375
- up_parent: bfloat16 [4096, 7168], P('var', 'tp'), may hold values from -0.09375 to 0.09375
- down_parent: bfloat16 [7168, 4096], P('tp', 'var'), may hold values from -0.0625 to 0.0625
- targets: bfloat16 [256, 4096], P('var', 'tp'), may hold values from -6 to 6
- widths: int32 [32], P('var'), may hold values from 1792 to 7168, as said below
- gains: float32 [32, 7168], P('var', 'tp'), may hold values from 0.25 to 2
Outputs:
- down_grad: bfloat16 [32, 7168, 4096], P('var', 'tp')
- gain_grad: float32 [32, 7168], P('var', 'tp')
Inputs may be any that keep to these rules, and one draw needn't show every extreme that they name: `widths`: every draw has a variant of exactly 7168 and one of exactly 1792 kept hidden units.
All inputs are finite; a program needn't handle non-finite values.
Results may differ from a plain program's by a relative error of at most 0.0059.
Values may be sent and summed in bfloat16 or wider, within the bound.
No kernel may reach another device: no remote copies, remote signals or barrier semaphores. Data moves between devices by JAX's collectives and lax.ppermute only.
A program may use at most 128 MiB of HBM per device.

v0:
```python
import jax
import jax.numpy as jnp
from jax import lax
from jax.sharding import PartitionSpec as P


def local(parent_inputs, gate_parent, up_parent, down_parent, targets, widths, gains):
    contract_rows = (((0,), (0,)), ((), ()))
    rows = parent_inputs.shape[1]
    local_ff = gate_parent.shape[1]
    feats = lax.all_gather(parent_inputs, "var", axis=0, tiled=True)
    gate_piece = lax.all_gather(gate_parent, "var", axis=0, tiled=True)
    up_piece = lax.all_gather(up_parent, "var", axis=0, tiled=True)
    gate_sum = lax.dot_general(feats, gate_piece, contract_rows, preferred_element_type=jnp.float32)
    up_sum = lax.dot_general(feats, up_piece, contract_rows, preferred_element_type=jnp.float32)
    raw = jax.nn.silu(gate_sum) * up_sum
    column = lax.axis_index("tp") * local_ff + lax.broadcasted_iota(jnp.int32, (1, local_ff), 1)
    kept = (column < widths[0]).astype(jnp.float32)
    hidden = (raw * gains * kept).astype(jnp.bfloat16)
    down_whole = lax.all_gather(down_parent, "var", axis=1, tiled=True)
    partial_value = jnp.dot(hidden, down_whole, preferred_element_type=jnp.float32)
    target_part = lax.all_gather(targets, "var", axis=0, tiled=True)
    output = lax.psum(partial_value, "tp")
    target_whole = lax.all_gather(target_part, "tp", axis=1, tiled=True)
    residual = (output - target_whole.astype(jnp.float32)).astype(jnp.bfloat16)
    scale = 1.0 / rows**0.5
    grad_down = lax.dot_general(hidden, residual, contract_rows, preferred_element_type=jnp.float32)
    grad_down = (grad_down * scale).astype(jnp.bfloat16)[None]
    back = lax.dot_general(
        residual, down_whole, (((1,), (1,)), ((), ())), preferred_element_type=jnp.float32
    )
    grad_gain = kept * jnp.sum(raw * back, axis=0, keepdims=True) * scale
    return (grad_down, grad_gain)


def solution(mesh):
    return jax.shard_map(
        local,
        mesh=mesh,
        in_specs=(
            P("var", None),
            P("var", "tp"),
            P("var", "tp"),
            P("tp", "var"),
            P("var", "tp"),
            P("var"),
            P("var", "tp"),
        ),
        out_specs=(P("var", "tp", None), P("var", "tp")),
        check_vma=False,
    )
```

profile of v0, /device:TPU:1, one launch (start us, length us, event | category | flops | bytes accessed | tf_op | source)
XLA Modules:
  0.0 589.8 jit_solution(13577693330374438191)
XLA Ops:
  7.2 0.0 all-gather.6.cloned.1.call-start
  7.2 0.7 all-gather.6.cloned.1.call-update
  7.9 0.0 all-gather.8.cloned.1.call-start
  7.9 0.7 all-gather.8.cloned.1.call-update
  8.6 0.0 all-gather.10.cloned.1.call-start
  8.7 0.7 all-gather.10.cloned.1.call-update
  9.4 0.0 all-gather.12.cloned.1.call-start
  9.4 0.5 all-gather.12.cloned.1.call-update
  10.0 0.0 all-gather.14.cloned.1.call-start
  10.0 49.5 %all_gather.22 = bf16[256,512]{1,0:T(8,128)(2,1)} all-gather(bf16[8,512]{1,0:T(8,128)(2,1)} %param.11), channel_id=1, replica_groups=mesh['var'=32,'tp'=8] {'var'}, dimensions={0}, use_global_device_ids=true | all-gather | bytes 270336 | tf_op jit(solution)/shard_map/all_gather | solution.py:22
  59.5 0.0 all-reduce.2.cloned.1.call-start
  60.2 0.7 reduce
  60.9 13.4 %all-gather.6.cloned.1.call-done = bf16[4096,256]{1,0:T(8,128)(2,1)} async-done(((bf16[128,256]{1,0:T(8,128)(2,1)}), bf16[4096,256]{1,0:T(8,128)(2,1)}) %all-gather.6.cloned.1.call-update) | async-done | bytes 2097168 | tf_op jit(solution)/shard_map/all_gather | solution.py:11
  74.4 69.0 %all-gather.8.cloned.1.call-done = bf16[4096,896]{1,0:T(8,128)(2,1)} async-done(((bf16[128,896]{1,0:T(8,128)(2,1)}), bf16[4096,896]{1,0:T(8,128)(2,1)}) %all-gather.8.cloned.1.call-update) | async-done | bytes 7340048 | tf_op jit(solution)/shard_map/all_gather | solution.py:12
  143.3 7.0 %fusion.5 = f32[256,896]{1,0:T(8,128)} fusion(bf16[4096,256]{1,0:T(8,128)(2,1)} %all-gather.6.cloned.1.call-done, bf16[4096,896]{1,0:T(8,128)(2,1)} %all-gather.8.cloned.1.call-done), kind=kOutput, calls=%fused_computation.12 | convolution fusion | flops 1879048192 | bytes 10354688 | tf_op jit(solution)/shard_map/dot_general | solution.py:14
  150.3 61.7 %all-gather.10.cloned.1.call-done = bf16[4096,896]{1,0:T(8,128)(2,1)} async-done(((bf16[128,896]{1,0:T(8,128)(2,1)}), bf16[4096,896]{1,0:T(8,128)(2,1)}) %all-gather.10.cloned.1.call-update) | async-done | bytes 7340048 | tf_op jit(solution)/shard_map/all_gather | solution.py:13
  212.1 5.7 convolution_multiply_fusion.1
  217.7 77.8 %all-gather.12.cloned.1.call-done = bf16[896,4096]{1,0:T(8,128)(2,1)} async-done(((bf16[896,128]{1,0:T(8,128)(2,1)}), bf16[896,4096]{1,0:T(8,128)(2,1)}) %all-gather.12.cloned.1.call-update) | async-done | bytes 7340048 | tf_op jit(solution)/shard_map/all_gather | solution.py:20
  295.5 7.4 %fusion.2 = f32[256,4096]{1,0:T(8,128)} fusion(bf16[896,4096]{1,0:T(8,128)(2,1)} %all-gather.12.cloned.1.call-done, f32[256,896]{1,0:T(8,128)S(1)} %convolution_multiply_fusion.1, f32[896]{0:T(1024)S(1)} %fusion.3, f32[896]{0:T(1024)S(1)} %reduce), kind=kOutput, calls=%fused_computation.7 | convolution fusion | flops 1879736320 | bytes 12459008 | tf_op jit(solution)/shard_map/dot_general | solution.py:21
  303.0 68.9 %all-gather.14.cloned.1.call-done = bf16[256,4096]{1,0:T(8,128)(2,1)} async-done(((bf16[256,512]{1,0:T(8,128)(2,1)}), bf16[256,4096]{1,0:T(8,128)(2,1)}) %all-gather.14.cloned.1.call-update) | async-done | bytes 2097168 | tf_op jit(solution)/shard_map/all_gather | solution.py:24
  371.9 197.8 %all-reduce.2.cloned.1.call-done = f32[256,4096]{1,0:T(8,128)} async-done(((f32[256,4096]{1,0:T(8,128)}), f32[256,4096]{1,0:T(8,128)}) %all-reduce.2.cloned.1.call-update) | async-done | bytes 4194320 | tf_op jit(solution)/shard_map/psum | solution.py:23
  569.7 7.4 %fusion.1 = f32[896]{0:T(1024)S(1)} fusion(f32[256,896]{1,0:T(8,128)S(1)} %convolution_multiply_fusion.1, bf16[896,4096]{1,0:T(8,128)(2,1)} %all-gather.12.cloned.1.call-done, f32[256,4096]{1,0:T(8,128)} %all-reduce.2.cloned.1.call-done, bf16[256,4096]{1,0:T(8,128)(2,1)} %all-gather.14.cloned.1.call-done), kind=kOutput, calls=%fused_computation.5 | convolution fusion | flops 1882651776 | bytes 14552576 | tf_op jit(solution)/shard_map/dot_general | solution.py:29
  577.1 0.6 fusion.4
  577.7 5.2 fusion
  (9 shorter events, 0.1 us)
Async XLA Ops:
  7.2 67.2 %all-gather.6.cloned.1.call-start = ((), (), s32[]{:S(2)}) async-start(), calls=%async_computation | async-start | bytes 2162688 | tf_op jit(solution)/shard_map/all_gather | solution.py:11
  7.9 135.4 %all-gather.8.cloned.1.call-start = ((), (), s32[]{:S(2)}) async-start(), calls=%async_computation.1 | async-start | bytes 7569408 | tf_op jit(solution)/shard_map/all_gather | solution.py:12
  8.6 203.4 %all-gather.10.cloned.1.call-start = ((), (), s32[]{:S(2)}) async-start(), calls=%async_computation.2 | async-start | bytes 7569408 | tf_op jit(solution)/shard_map/all_gather | solution.py:13
  9.4 286.1 %all-gather.12.cloned.1.call-start = ((), (), s32[]{:S(2)}) async-start(), calls=%async_computation.3 | async-start | bytes 7569408 | tf_op jit(solution)/shard_map/all_gather | solution.py:20
  10.0 361.9 %all-gather.14.cloned.1.call-start = ((), (), s32[]{:S(2)}) async-start(), calls=%async_computation.5 | async-start | bytes 2359296 | tf_op jit(solution)/shard_map/all_gather | solution.py:24
  59.5 510.2 %all-reduce.2.cloned.1.call-start = ((), (), s32[]{:S(2)}) async-start(), calls=%async_computation.4 | async-start | bytes 8388608 | tf_op jit(solution)/shard_map/psum | solution.py:23
  74.4 137.7 %copy-start = (bf16[4096,256]{1,0:T(8,128)(2,1)S(1)}, bf16[4096,256]{1,0:T(8,128)(2,1)}, u32[]{:S(2)}) copy-start(bf16[4096,256]{1,0:T(8,128)(2,1)} %all-gather.6.cloned.1.call-done) | copy-start | bytes 6291460
  371.9 205.8 %copy-start.2 = (bf16[256,4096]{1,0:T(8,128)(2,1)S(1)}, bf16[256,4096]{1,0:T(8,128)(2,1)}, u32[]{:S(2)}) copy-start(bf16[256,4096]{1,0:T(8,128)(2,1)} %all-gather.14.cloned.1.call-done) | copy-start | bytes 6291460
  569.7 8.1 %copy-start.1 = (f32[256,4096]{1,0:T(8,128)S(1)}, f32[256,4096]{1,0:T(8,128)}, u32[]{:S(2)}) copy-start(f32[256,4096]{1,0:T(8,128)} %all-reduce.2.cloned.1.call-done) | copy-start | bytes 12582916
Sparse Core Ops, SparseCore 0:
  9.9 64.4 all-gather.5
  76.2 67.0 all-gather.7
  145.2 66.8 all-gather.9
  213.7 81.7 all-gather.11
  297.8 74.0 all-gather.13
  375.0 194.6 all-reduce.1
where the time goes:
time: 590 us
  waiting for transfers between devices  491 us (83%)
  blocking collectives  49.5 us (8%)
  matrix products  32.8 us (6%)
  between operations  14.8 us (3%)
    psum x1, waiting for transfers between devices, local(): output = lax.psum(partial_value, 'tp')  198 us
    all_gather x1, waiting for transfers between devices, local(): down_whole = lax.all_gather(down_parent, 'var', axis=1, tiled=True)  77.8 us
    all_gather x1, waiting for transfers between devices, local(): gate_piece = lax.all_gather(gate_parent, 'var', axis=0, tiled=True)  69 us
    all_gather x1, waiting for transfers between devices, local(): target_whole = lax.all_gather(target_part, 'tp', axis=1, tiled=True)  68.9 us
    all_gather x1, waiting for transfers between devices, local(): up_piece = lax.all_gather(up_parent, 'var', axis=0, tiled=True)  61.7 us
    all_gather x1, blocking collectives, local(): target_part = lax.all_gather(targets, 'var', axis=0, tiled=True)  49.5 us
    all_gather x1, waiting for transfers between devices, local(): feats = lax.all_gather(parent_inputs, 'var', axis=0, tiled=True)  13.4 us
  transfers between devices with their start and end apart: 6, of which 6 were waited for; matrix products, arithmetic and copies ran while one was open for 4% of the time, Pallas kernels for 0%

commit v1 on v0

--- a/solution.py
+++ b/solution.py
@@ -1,7 +1,15 @@
+import functools
 import jax
 import jax.numpy as jnp
 from jax import lax
 from jax.sharding import PartitionSpec as P
+
+
+def marks_remake(my_tile, lane_axis):
+    return jnp.sum(lax.all_gather(my_tile, lane_axis), 0)
+
+
+take_the_column = functools.partial(marks_remake, lane_axis="tp")
 
 
 def local(parent_inputs, gate_parent, up_parent, down_parent, targets, widths, gains):
@@ -20,7 +28,7 @@
     down_whole = lax.all_gather(down_parent, "var", axis=1, tiled=True)
     partial_value = jnp.dot(hidden, down_whole, preferred_element_type=jnp.float32)
     target_part = lax.all_gather(targets, "var", axis=0, tiled=True)
-    output = lax.psum(partial_value, "tp")
+    output = take_the_column(partial_value)
     target_whole = lax.all_gather(target_part, "tp", axis=1, tiled=True)
     residual = (output - target_whole.astype(jnp.float32)).astype(jnp.bfloat16)
     scale = 1.0 / rows**0.5

time: 590 us -> 970 us (1.64)
  waiting for transfers between devices: 491 us -> 857 us
  other arithmetic: 1.3 us -> 15.5 us
    all_gather x0 -> x1, waiting for transfers between devices: none -> 523 us  [marks_remake(): return jnp.sum(lax.all_gather(my_tile, lane_axis), 0)]
    psum x1 -> x0, waiting for transfers between devices: 198 us -> none  [local(): output = lax.psum(partial_value, 'tp')]
    all_gather x1, waiting for transfers between devices: 13.4 us -> 62.9 us  [local(): feats = lax.all_gather(parent_inputs, 'var', axis=0, tiled=True)]
    reduce_sum x0 -> x1, other arithmetic: none -> 14.2 us  [marks_remake(): return jnp.sum(lax.all_gather(my_tile, lane_axis), 0)]
  transfers between devices with their start and end apart: 6 -> 6, of which waited for: 6 -> 6; matrix products, arithmetic and copies ran while one was open for 4% -> 3% of each run, Pallas kernels for 0% -> 0%
where the time goes in v1:
time: 970 us
  waiting for transfers between devices  857 us (88%)
  blocking collectives  49 us (5%)
  matrix products  32.8 us (3%)
  other arithmetic  15.5 us (2%)
  between operations  14.8 us (2%)
    all_gather x1, waiting for transfers between devices, marks_remake(): return jnp.sum(lax.all_gather(my_tile, lane_axis), 0)  523 us
    all_gather x1, waiting for transfers between devices, local(): down_whole = lax.all_gather(down_parent, 'var', axis=1, tiled=True)  77.8 us
    all_gather x1, waiting for transfers between devices, local(): gate_piece = lax.all_gather(gate_parent, 'var', axis=0, tiled=True)  68.9 us
    all_gather x1, waiting for transfers between devices, local(): feats = lax.all_gather(parent_inputs, 'var', axis=0, tiled=True)  62.9 us
    all_gather x1, waiting for transfers between devices, local(): up_piece = lax.all_gather(up_parent, 'var', axis=0, tiled=True)  61.7 us
    all_gather x1, waiting for transfers between devices, local(): target_whole = lax.all_gather(target_part, 'tp', axis=1, tiled=True)  59.7 us
    all_gather x1, blocking collectives, local(): target_part = lax.all_gather(targets, 'var', axis=0, tiled=True)  49 us
  transfers between devices with their start and end apart: 6, of which 6 were waited for; matrix products, arithmetic and copies ran while one was open for 3% of the time, Pallas kernels for 0%

profile of v1, /device:TPU:1, one launch (start us, length us, event | category | flops | bytes accessed | tf_op | source)
XLA Modules:
  0.0 970.0 jit_solution(7862191432472152313)
XLA Ops:
  7.2 0.7 all-gather.8.cloned.1.call-update
  7.9 0.0 all-gather.10.cloned.1.call-start
  7.9 0.7 all-gather.10.cloned.1.call-update
  8.6 0.0 all-gather.12.cloned.1.call-start
  8.7 0.7 all-gather.12.cloned.1.call-update
  9.4 0.5 all-gather.14.cloned.1.call-update
  10.0 0.0 all-gather.18.cloned.1.call-start
  10.7 0.7 reduce
  11.4 62.9 %all-gather.8.cloned.1.call-done = bf16[4096,256]{1,0:T(8,128)(2,1)} async-done(((bf16[128,256]{1,0:T(8,128)(2,1)}), bf16[4096,256]{1,0:T(8,128)(2,1)}) %all-gather.8.cloned.1.call-update) | async-done | bytes 2097168 | tf_op jit(solution)/shard_map/all_gather | solution.py:19
  74.3 68.9 %all-gather.10.cloned.1.call-done = bf16[4096,896]{1,0:T(8,128)(2,1)} async-done(((bf16[128,896]{1,0:T(8,128)(2,1)}), bf16[4096,896]{1,0:T(8,128)(2,1)}) %all-gather.10.cloned.1.call-update) | async-done | bytes 7340048 | tf_op jit(solution)/shard_map/all_gather | solution.py:20
  143.2 7.0 fusion.5
  150.2 61.7 %all-gather.12.cloned.1.call-done = bf16[4096,896]{1,0:T(8,128)(2,1)} async-done(((bf16[128,896]{1,0:T(8,128)(2,1)}), bf16[4096,896]{1,0:T(8,128)(2,1)}) %all-gather.12.cloned.1.call-update) | async-done | bytes 7340048 | tf_op jit(solution)/shard_map/all_gather | solution.py:21
  211.9 5.7 convolution_multiply_fusion.1
  217.6 77.8 %all-gather.14.cloned.1.call-done = bf16[896,4096]{1,0:T(8,128)(2,1)} async-done(((bf16[896,128]{1,0:T(8,128)(2,1)}), bf16[896,4096]{1,0:T(8,128)(2,1)}) %all-gather.14.cloned.1.call-update) | async-done | bytes 7340048 | tf_op jit(solution)/shard_map/all_gather | solution.py:28
  295.4 7.4 fusion.2
  302.8 0.0 all-gather.16.cloned.1.call-start
  302.9 0.6 copy-done.3
  303.5 49.0 %all_gather.30 = bf16[256,512]{1,0:T(8,128)(2,1)} all-gather(bf16[8,512]{1,0:T(8,128)(2,1)S(1)} %copy-done.3), channel_id=1, replica_groups=mesh['var'=32,'tp'=8] {'var'}, dimensions={0}, use_global_device_ids=true | all-gather | bytes 270336 | tf_op jit(solution)/shard_map/all_gather | solution.py:30
  352.5 523.4 %all-gather.18.cloned.1.call-done = f32[2048,4096]{1,0:T(8,128)} async-done(((f32[256,4096]{1,0:T(8,128)}), f32[2048,4096]{1,0:T(8,128)}) %all-gather.18.cloned.1.call-update) | async-done | bytes 33554448 | tf_op jit(solution)/shard_map/all_gather | solution.py:9
  876.0 14.2 %reduce_sum.20 = f32[256,4096]{1,0:T(8,128)} reduce(f32[8,256,4096]{2,1,0:T(8,128)} %bitcast.12, f32[]{:T(128)} %constant.4.clone.1), dimensions={0}, to_apply=%region_0.1 | reduce | flops 7340032 | bytes 37748740 | tf_op jit(solution)/shard_map/reduce_sum | solution.py:9
  890.1 59.7 %all-gather.16.cloned.1.call-done = bf16[256,4096]{1,0:T(8,128)(2,1)} async-done(((bf16[256,512]{1,0:T(8,128)(2,1)}), bf16[256,4096]{1,0:T(8,128)(2,1)}) %all-gather.16.cloned.1.call-update) | async-done | bytes 2097168 | tf_op jit(solution)/shard_map/all_gather | solution.py:32
  949.9 7.4 fusion.1
  957.3 0.6 fusion.4
  957.9 5.2 fusion
  (12 shorter events, 0.1 us)
Async XLA Ops:
  7.2 67.1 %all-gather.8.cloned.1.call-start = ((), (), s32[]{:S(2)}) async-start(), calls=%async_computation | async-start | bytes 2162688 | tf_op jit(solution)/shard_map/all_gather | solution.py:19
  7.9 135.3 %all-gather.10.cloned.1.call-start = ((), (), s32[]{:S(2)}) async-start(), calls=%async_computation.1 | async-start | bytes 7569408 | tf_op jit(solution)/shard_map/all_gather | solution.py:20
  8.6 203.3 %all-gather.12.cloned.1.call-start = ((), (), s32[]{:S(2)}) async-start(), calls=%async_computation.2 | async-start | bytes 7569408 | tf_op jit(solution)/shard_map/all_gather | solution.py:21
  9.4 286.0 %all-gather.14.cloned.1.call-start = ((), (), s32[]{:S(2)}) async-start(), calls=%async_computation.3 | async-start | bytes 7569408 | tf_op jit(solution)/shard_map/all_gather | solution.py:28
  10.0 866.0 %all-gather.18.cloned.1.call-start = ((), (), s32[]{:S(2)}) async-start(), calls=%async_computation.5 | async-start | bytes 37748736 | tf_op jit(solution)/shard_map/all_gather | solution.py:9
  74.3 137.6 %copy-start.1 = (bf16[4096,256]{1,0:T(8,128)(2,1)S(1)}, bf16[4096,256]{1,0:T(8,128)(2,1)}, u32[]{:S(2)}) copy-start(bf16[4096,256]{1,0:T(8,128)(2,1)} %all-gather.8.cloned.1.call-done) | copy-start | bytes 6291460
  302.8 0.7 copy-start.3
  302.8 647.0 %all-gather.16.cloned.1.call-start = ((), (), s32[]{:S(2)}) async-start(), calls=%async_computation.4 | async-start | bytes 2359296 | tf_op jit(solution)/shard_map/all_gather | solution.py:32
  949.9 8.1 copy-start
  949.9 8.1 copy-start.2
Sparse Core Ops, SparseCore 0:
  9.9 64.3 all-gather.7
  76.1 67.0 all-gather.9
  145.0 66.8 all-gather.11
  213.5 81.7 all-gather.13
  302.9 572.9 all-gather.17
  878.3 71.5 all-gather.15
